TPU v7x, 768 devices: a whole 4x8x12 slice. The times are simulated.
768 devices in a mesh: group: 16 (over x, z_hi, core), replica: 48 (over z_lo, y).
Axes of the slice: x: 4, y: 8, z: 12 (z_hi: 2, z_lo: 6; z = z_hi * 6 + z_lo), core: 2. Of those that a mesh axis runs over, the one named last changes fastest.
Arguments:
- grad_parts: bfloat16 [48, 48, 512, 512], P('replica', None, 'group'), may hold values from -1 to 1
- owner_order: int32 [48], replicated, may hold values from 0 to 47, each once
- step_count: int32 [1], replicated, may hold values from 1 to 12
- stat_old: float32 [48, 512, 512], P('replica'), as said below
- root_old: bfloat16 [48, 512, 512], P('replica'), may hold values from -0.25 to 0.25
Outputs:
- update: bfloat16 [48, 512, 512], P(None, 'group')
- stat_new: float32 [48, 512, 512], P('replica')
- root_new: bfloat16 [48, 512, 512], P('replica')
Inputs may be any that keep to these rules, and one draw needn't show every extreme that they name: `stat_old`: each matrix is symmetric positive definite.
All inputs are finite; a program needn't handle non-finite values.
Results may differ from a plain program's by a relative error of at most 0.001.
The roundings to bfloat16 on the way count: a program that leaves them out, or rounds other values in their place, can miss the bound.
Values may be sent and summed in bfloat16 or wider, within the bound.
A program may use at most 32 MiB of HBM per device.

v0:
```python
import jax
import jax.numpy as jnp
from jax import lax
from jax.sharding import PartitionSpec as P

ITERS = 3


decay_rate = 0.95
epsilon = 0.001


def newton(shifted):
    identity = jnp.eye(shifted.shape[0], dtype=jnp.float32)
    frobenius = jnp.sqrt(jnp.sum(shifted * shifted))
    coupled = shifted / frobenius
    root_iter = identity * frobenius ** (-0.25)
    for repeat in range(ITERS):
        factor = (5.0 * identity - coupled) * 0.25
        root_iter = jnp.dot(root_iter, factor, precision=lax.Precision.HIGHEST)
        if repeat + 1 < ITERS:
            factor_sq = jnp.dot(factor, factor, precision=lax.Precision.HIGHEST)
            factor_quad = jnp.dot(factor_sq, factor_sq, precision=lax.Precision.HIGHEST)
            coupled = jnp.dot(factor_quad, coupled, precision=lax.Precision.HIGHEST)
    return root_iter


def local(grad_parts, owner_order, step_count, stat_old, root_old):
    local_grads = grad_parts[0]
    ordered = local_grads[owner_order]
    owned = lax.psum_scatter(
        ordered.astype(jnp.float32), "replica", scatter_dimension=0, tiled=True
    )
    partial_gram = jnp.einsum("bri,brj->bij", owned, owned, precision=lax.Precision.HIGHEST)
    products = jnp.einsum(
        "bri,bij->brj", owned.astype(jnp.bfloat16), root_old, preferred_element_type=jnp.float32
    )
    partial_norm = jnp.sum(products * products, axis=(1, 2))
    gram_matrix, update_norm = lax.psum((partial_gram, partial_norm), "group")
    grad_norm = jnp.trace(gram_matrix, axis1=1, axis2=2)
    graft_scale = jnp.sqrt(grad_norm / (update_norm + 1e-06))
    scaled = (graft_scale[:, None, None] * products).astype(jnp.bfloat16)
    gathered = lax.all_gather(scaled, "replica", axis=0, tiled=True)
    update = jnp.zeros_like(gathered).at[owner_order].set(gathered)
    stat_new = decay_rate * stat_old + (1.0 - decay_rate) * gram_matrix
    correction = 1.0 / (1.0 - decay_rate ** step_count[0].astype(jnp.float32))
    shifted = stat_new * correction + epsilon * jnp.eye(stat_new.shape[1], dtype=jnp.float32)
    root_new = lax.map(newton, shifted).astype(jnp.bfloat16)
    return (update, stat_new, root_new)


def solution(mesh):
    placed = (
        P("replica", None, "group", None),
        P(),
        P(),
        P("replica", None, None),
        P("replica", None, None),
    )
    return jax.shard_map(
        local,
        mesh=mesh,
        in_specs=placed,
        out_specs=(P(None, "group", None), P("replica", None, None), P("replica", None, None)),
        check_vma=False,
    )
```

profile of v0, /device:TPU:4, one launch (start us, length us, event | category | flops | bytes accessed | tf_op | source)
XLA Modules:
  0.0 864.6 jit_solution(16502267337760494657)
XLA Ops:
  7.2 0.0 copy-start
  7.2 0.0 reduce-scatter.2.cloned.1.call-start
  7.2 0.8 compare_select_fusion
  8.0 0.6 copy-done
  8.6 0.7 gather_fusion
  9.3 2.1 convert_element_type.25
  11.4 0.0 reduce-scatter.2.cloned.1.call-update
  11.4 0.0 copy-start.4
  11.4 0.0 copy-start.2
  11.4 0.0 all-reduce.2.cloned.1.call-start
  11.5 321.3 %reduce-scatter.2.cloned.1.call-done = f32[1,32,512]{2,1,0:T(8,128)} async-done(((f32[48,32,512]{2,1,0:T(8,128)}), f32[1,32,512]{2,1,0:T(8,128)}) %reduce-scatter.2.cloned.1.call-update) | async-done | bytes 65552 | tf_op jit(solution)/shard_map/reduce_scatter | solution.py:31
  332.8 0.0 copy-start.5
  332.8 2.9 convolution_bitcast_fusion
  335.7 0.0 all-reduce.2.cloned.1.call-update
  335.8 0.0 all-gather.3.cloned.1.call-start
  336.5 0.0 copy-done.4
  336.5 0.0 copy-done.5
  336.6 0.8 multiply_reduce_fusion.1
  337.4 48.6 %psum.15 = f32[1]{0:T(128)} all-reduce(f32[1]{0:T(128)} %bitcast.6), channel_id=1, replica_groups=mesh['group'=16,'replica'=48] {'group'}, use_global_device_ids=true, to_apply=%region_4.5 | all-reduce | flops 1 | bytes 8 | tf_op jit(solution)/shard_map/psum | solution.py:39
  386.6 162.4 %all-reduce.2.cloned.1.call-done = f32[1,512,512]{2,1,0:T(8,128)} async-done(((f32[1,512,512]{2,1,0:T(8,128)}), f32[1,512,512]{2,1,0:T(8,128)}) %all-reduce.2.cloned.1.call-update) | async-done | bytes 1048592 | tf_op jit(solution)/shard_map/psum | solution.py:39
  549.0 0.0 copy-done.2
  549.0 3.0 multiply_reduce_fusion
  552.8 0.6 multiply_convert_fusion
  553.4 0.0 all-gather.3.cloned.1.call-update
  554.2 3.7 fusion.6
  557.9 0.0 copy-start.3
  557.9 1.8 fusion.53
  559.7 0.0 copy-done.3
  559.7 1.9 fusion.8
  561.7 1.9 fusion.16
  563.6 1.8 fusion.54
  565.4 1.8 fusion
  567.3 2.1 fusion.3
  569.4 1.9 fusion.18
  571.3 2.6 fusion.1
  574.0 277.7 %all-gather.3.cloned.1.call-done = bf16[1536,512]{1,0:T(8,128)(2,1)} async-done(((bf16[32,512]{1,0:T(8,128)(2,1)}), bf16[1536,512]{1,0:T(8,128)(2,1)}) %all-gather.3.cloned.1.call-update) | async-done | bytes 1572880 | tf_op jit(solution)/shard_map/all_gather | solution.py:43
  851.7 0.2 broadcast_in_dim.20
  851.8 5.1 scatter_fusion
  856.9 0.0 copy-start.1
  857.0 1.1 copy-done.1
  (1 shorter events, 0.0 us)
Async XLA Ops:
  7.2 1.4 copy-start
  7.2 325.6 %reduce-scatter.2.cloned.1.call-start = ((), (), s32[]{:S(2)}) async-start(), calls=%async_computation.1 | async-start | bytes 3211264 | tf_op jit(solution)/shard_map/reduce_scatter | solution.py:31
  11.4 325.2 %copy-start.4 = (bf16[1,512,512]{2,1,0:T(8,128)(2,1)S(1)}, bf16[1,512,512]{2,1,0:T(8,128)(2,1)}, u32[]{:S(2)}) copy-start(bf16[1,512,512]{2,1,0:T(8,128)(2,1)} %param.9) | copy-start | bytes 1572868
  11.4 537.7 %copy-start.2 = (f32[1,512,512]{2,1,0:T(8,128)S(1)}, f32[1,512,512]{2,1,0:T(8,128)}, u32[]{:S(2)}) copy-start(f32[1,512,512]{2,1,0:T(8,128)} %param.8) | copy-start | bytes 3145732
  11.4 537.6 %all-reduce.2.cloned.1.call-start = ((), (), s32[]{:S(2)}) async-start(), calls=%async_computation.2 | async-start | bytes 2097152 | tf_op jit(solution)/shard_map/psum | solution.py:39
  332.8 3.8 copy-start.5
  335.8 515.9 %all-gather.3.cloned.1.call-start = ((), (), s32[]{:S(2)}) async-start(), calls=%async_computation.3 | async-start | bytes 1605632 | tf_op jit(solution)/shard_map/all_gather | solution.py:43
  557.9 1.9 copy-start.3
  856.9 1.1 copy-start.1
Sparse Core Ops, SparseCore 0:
  11.5 321.2 reduce-scatter.1
  336.9 212.0 all-reduce.1
  553.6 298.0 all-gather.2
where the time goes:
time: 865 us
  waiting for transfers between devices  761 us (88%)
  blocking collectives  48.6 us (6%)
  matrix products  23.5 us (3%)
  between operations  16.7 us (2%)
    reduce_scatter x1, waiting for transfers between devices, local(): lax.psum_scatter(ordered.astype(jnp.float32), 'replica', scatter_dimensio...  321 us
    all_gather x1, waiting for transfers between devices, local(): gathered = lax.all_gather(scaled, 'replica', axis=0, tiled=True)  278 us
    psum x1, waiting for transfers between devices, local(): gram_matrix, update_norm = lax.psum((partial_gram, partial_norm), 'group')  162 us
    psum x1, blocking collectives, local(): gram_matrix, update_norm = lax.psum((partial_gram, partial_norm), 'group')  48.6 us
  transfers between devices with their start and end apart: 3, of which 3 were waited for; matrix products, arithmetic and copies ran while one was open for 2% of the time, Pallas kernels for 0%

commit v1 on v0

v1 whole, which is shorter than its diff:
```python
import jax
import jax.numpy as jnp
from jax import lax
from jax.experimental import pallas as pl
from jax.experimental.pallas import tpu as pltpu
from jax.sharding import PartitionSpec as P

ITERS = 3
DECAY = 0.95
EPS = 0.001
NY, NZ = 8, 6
NB, ROWS, W = 48, 32, 512
CA = 384
F32, BF16 = jnp.float32, jnp.bfloat16


def split(value):
    high = value.astype(BF16)
    return high, (value - high.astype(F32)).astype(BF16)


def eye_block(first, rows):
    row = lax.broadcasted_iota(jnp.int32, (rows, W), 0) + first
    return row == lax.broadcasted_iota(jnp.int32, (rows, W), 1)


def kernel(
    order, inverse, step, gp, stat_hbm, root_hbm,
    update, stat_out, root_out,
    raw_y, raw_y_in, sum_y, sum_y_in, raw_z, raw_z_in, tot_z, tot_z_in, fin_z, fin_z_in,
    owned, norms, norms_in, rows_all, stat_v, root_v, gathered,
    th, tl, mh, ml, qh, ql, xh, xl, shifted,
    y_s, y_r, zr_s, zr_r, zt_s, zt_r, zf_s, zf_r, nb_s, nb_r, gx_s, gx_r, gc_s, gc_r, gz_s, gz_r,
    cz_s, cz_r, cy_s, cy_r, loc,
):
    g, r = lax.axis_index("group"), lax.axis_index("replica")
    x, zh, c = g // 4, lax.rem(g // 2, 2), lax.rem(g, 2)
    z, y = r // NY, lax.rem(r, NY)

    def gid(xx, hh, cc):
        return xx * 4 + hh * 2 + cc

    def yy(d):
        return lax.rem(y + d + NY, NY)

    def zz(d):
        return lax.rem(z + d, NZ)

    def at_y(d):
        return g, z * NY + yy(d)

    def at_z(k):
        return g, zz(k + 1) * NY + y

    started = []

    def describe(src, dst, ss, rs, dev):
        return pltpu.make_async_remote_copy(
            src_ref=src, dst_ref=dst, send_sem=ss, recv_sem=rs,
            device_id=dev, device_id_type=pl.DeviceIdType.MESH,
        )

    def put(src, dst, ss, rs, dev):
        copy = describe(src, dst, ss, rs, dev)
        copy.start()
        started.append(copy)

    def arrived(dst, ss, rs, dev):
        describe(dst, dst, ss, rs, dev).wait_recv()

    stat_copy = pltpu.make_async_copy(stat_hbm.at[0], stat_v, loc.at[0])
    root_copy = pltpu.make_async_copy(root_hbm.at[0], root_v, loc.at[1])
    stat_copy.start()
    root_copy.start()

    barrier = pltpu.get_barrier_semaphore()
    peers = [at_y(d) for d in range(1, NY)] + [at_z(k) for k in range(NZ - 1)]
    peers += [(lax.rem(g + m, 16), r) for m in range(1, 16)]
    for dev in peers:
        pl.semaphore_signal(barrier, inc=1, device_id=dev, device_id_type=pl.DeviceIdType.MESH)

    def block(k, d, first, width):
        return gp[0, order[zz(k + 1) * NY + yy(d)], :, pl.ds(first, width)]

    def reach(way, k):
        return 4 if (way + k) % 2 == 0 else 3

    step_of = (1, -1)
    for k in range(NZ):
        for way in range(2):
            raw_y[way, k] = block(k, step_of[way] * reach(way, k), 0, CA)
    for k in range(NZ - 1):
        for d in range(NY):
            raw_z[k, d] = block(k, d, CA, W - CA)
    pl.semaphore_wait(barrier, len(peers))

    def near(way):
        return at_y(step_of[way])

    for k in range(NZ):
        for way in range(2):
            at = reach(way, k) - 1
            put(raw_y.at[way, k], raw_y_in.at[way, k], y_s.at[way, k, at], y_r.at[way, k, at], near(way))
    for k in range(NZ - 1):
        put(raw_z.at[k], raw_z_in.at[k], zr_s.at[k], zr_r.at[k], at_z(k))

    def incoming(way, k, d):
        if d == reach(way, k):
            arrived(raw_y_in.at[way, k], y_s.at[way, k, d - 1], y_r.at[way, k, d - 1], near(way))
            return raw_y_in[way, k].astype(F32)
        arrived(sum_y_in.at[way, k, d - 1], y_s.at[way, k, d - 1], y_r.at[way, k, d - 1], near(way))
        return sum_y_in[way, k, d - 1]

    def pass_on(d):
        for k in range(NZ):
            for way in range(2):
                if d < reach(way, k):
                    total = incoming(way, k, d + 1) + block(k, step_of[way] * d, 0, CA).astype(F32)
                    sum_y[way, k, d - 1] = total
                    put(sum_y.at[way, k, d - 1], sum_y_in.at[way, k, d - 1], y_s.at[way, k, d - 1], y_r.at[way, k, d - 1], near(way))

    pass_on(3)
    pass_on(2)
    for k in range(NZ - 1):
        arrived(raw_z_in.at[k], zr_s.at[k], zr_r.at[k], at_z(k))
    for d in range(NY):
        total = block(NZ - 1, d, CA, W - CA).astype(F32)
        for k in range(NZ - 1):
            total += raw_z_in[k, d].astype(F32)
        tot_z[d] = total
        if d:
            put(tot_z.at[d], tot_z_in.at[d - 1], zt_s.at[d - 1], zt_r.at[d - 1], at_y(d))
    pass_on(1)
    for k in range(NZ):
        total = incoming(0, k, 1) + incoming(1, k, 1) + block(k, 0, 0, CA).astype(F32)
        if k < NZ - 1:
            fin_z[k] = total
            put(fin_z.at[k], fin_z_in.at[k], zf_s.at[k], zf_r.at[k], at_z(k))
        else:
            mine = total
    for k in range(NZ - 1):
        arrived(fin_z_in.at[k], zf_s.at[k], zf_r.at[k], at_z(k))
        mine += fin_z_in[k]
    owned[:, 0:CA] = mine
    mine = tot_z[0]
    for d in range(NY - 1):
        arrived(tot_z_in.at[d], zt_s.at[d], zt_r.at[d], at_y(1))
        mine += tot_z_in[d]
    owned[:, CA:W] = mine

    root_copy.wait()
    products = jnp.dot(owned[...].astype(BF16), root_v[...], preferred_element_type=F32)
    mine = owned[...]
    grad_norm = jnp.sum(jnp.sum(mine * mine, axis=1, keepdims=True), axis=0, keepdims=True)
    update_norm = jnp.sum(jnp.sum(products * products, axis=1, keepdims=True), axis=0, keepdims=True)
    upper = lax.broadcasted_iota(jnp.int32, (8, 128), 0) < 4
    norms[...] = jnp.where(upper, grad_norm, update_norm)
    for m in range(1, 16):
        put(norms, norms_in.at[m - 1], nb_s.at[m - 1], nb_r.at[m - 1], (lax.rem(g + m, 16), r))

    rows_all[g] = mine

    def xat(m):
        return lax.rem(x + m, 4)

    far, sib = gid(x, 1 - zh, c), gid(x, zh, 1 - c)
    put(rows_all.at[g], rows_all.at[g], gz_s, gz_r, (far, r))
    for m in (1, 3, 2):
        put(rows_all.at[g], rows_all.at[g], gx_s.at[0, m], gx_r.at[0, m], (gid(xat(m), zh, c), r))
    put(rows_all.at[g], rows_all.at[g], gc_s.at[0, 0], gc_r.at[0, 0], (sib, r))

    total = norms[...]
    for m in range(15):
        arrived(norms_in.at[m], nb_s.at[m], nb_r.at[m], (sib, r))
        total += norms_in[m]
    graft = jnp.sqrt(total[0:1, 0:1] / (total[4:5, 0:1] + 1e-06))
    own_slot = z * NY + y
    gathered[own_slot] = (graft * products).astype(BF16)

    for k in range(NZ - 1):
        put(gathered.at[own_slot], gathered.at[own_slot], cz_s.at[k], cz_r.at[k], at_z(k))

    def from_z(k):
        return gathered.at[lax.rem(z + NZ - 1 - k, NZ) * NY + y]

    def slot_from(k, way, hops):
        zs = z if k == NZ - 1 else lax.rem(z + NZ - 1 - k, NZ)
        return gathered.at[zs * NY + yy(-step_of[way] * hops)]

    def hop(k, h):
        for way in range(2):
            if 0 < h <= reach(way, k):
                arrived(slot_from(k, way, h), cy_s.at[way, k, h - 1], cy_r.at[way, k, h - 1], near(way))
            if h < reach(way, k):
                ref = slot_from(k, way, h)
                put(ref, ref, cy_s.at[way, k, h], cy_r.at[way, k, h], near(way))

    def first(k):
        if k < NZ - 1:
            arrived(from_z(k), cz_s.at[k], cz_r.at[k], at_z(k))
        hop(k, 0)

    first(5)
    arrived(rows_all.at[far], gz_s, gz_r, (far, r))
    for m in (1, 3, 2):
        put(rows_all.at[far], rows_all.at[far], gx_s.at[1, m], gx_r.at[1, m], (gid(xat(m), zh, c), r))
    put(rows_all.at[far], rows_all.at[far], gc_s.at[1, 0], gc_r.at[1, 0], (sib, r))
    first(0)
    first(4)
    first(1)
    first(3)
    first(2)
    for h in range(1, 5):
        for k in (5, 0, 4, 1, 3, 2):
            hop(k, h)

    for half in range(2):
        hh = zh if half == 0 else 1 - zh
        for m in (1, 3, 2):
            slot = gid(lax.rem(x + 4 - m, 4), hh, c)
            arrived(rows_all.at[slot], gx_s.at[half, m], gx_r.at[half, m], (sib, r))
            put(rows_all.at[slot], rows_all.at[slot], gc_s.at[half, m], gc_r.at[half, m], (sib, r))

    def permute(b, carry):
        update[b] = gathered[inverse[b]]
        return carry

    lax.fori_loop(0, NB, permute, 0)

    for half in range(2):
        hh = zh if half == 0 else 1 - zh
        for m in range(4):
            slot = gid(lax.rem(x + 4 - m, 4), hh, 1 - c)
            arrived(rows_all.at[slot], gc_s.at[half, m], gc_r.at[half, m], (sib, r))

    high, low = split(rows_all[...].reshape(16 * ROWS, W))
    th[...] = high
    tl[...] = low

    def rows_dot(a, b):
        return lax.dot_general(a, b, (((0,), (0,)), ((), ())), preferred_element_type=F32)

    gram = rows_dot(th[...], th[...]) + rows_dot(th[...], tl[...]) + rows_dot(tl[...], th[...])
    stat_copy.wait()
    stat_new = DECAY * stat_v[...] + (1.0 - DECAY) * gram
    stat_out[0] = stat_new
    count = step[0]
    power = jnp.float32(1.0)
    for n in range(12):
        power = jnp.where(n < count, power * DECAY, power)
    correction = 1.0 / (1.0 - jnp.full((8, 128), power, F32))
    value = stat_new * correction[0:1, 0:1] + jnp.where(eye_block(0, W), EPS, 0.0)
    shifted[...] = value
    square = jnp.sum(jnp.sum(value * value, axis=1, keepdims=True), axis=0, keepdims=True)
    frobenius = jnp.sqrt(square)
    scale = 1.0 / jnp.sqrt(jnp.sqrt(frobenius))

    half_rows = W // 2

    def factor_of(i, coupled):
        rows = pl.ds(i * half_rows, half_rows)
        mh[rows], ml[rows] = split(coupled)
        factor = (jnp.where(eye_block(i * half_rows, half_rows), 5.0, 0.0) - coupled) * 0.25
        return rows, factor

    def product(a_high, a_low, b_high, b_low, give):
        for i in range(2):
            rows = pl.ds(i * half_rows, half_rows)
            out = jnp.dot(a_high[rows], b_high[...], preferred_element_type=F32)
            out += jnp.dot(a_high[rows], b_low[...], preferred_element_type=F32)
            out += jnp.dot(a_low[rows], b_high[...], preferred_element_type=F32)
            give(i, rows, out)

    def keep(high_ref, low_ref):
        def give(i, rows, out):
            high_ref[rows], low_ref[rows] = split(out)
        return give

    for i in range(2):
        rows, factor = factor_of(i, shifted[pl.ds(i * half_rows, half_rows)] / frobenius)
        th[rows], tl[rows] = split(factor)
        xh[rows], xl[rows] = th[rows], tl[rows]
    for repeat in range(ITERS):
        if repeat:
            if repeat + 1 < ITERS:
                product(xh, xl, th, tl, keep(qh, ql))
                xh[...], xl[...] = qh[...], ql[...]
            else:
                def finish(i, rows, out):
                    root_out[0, rows] = (out * scale).astype(BF16)
                product(xh, xl, th, tl, finish)
        if repeat + 1 < ITERS:
            product(th, tl, th, tl, keep(qh, ql))
            product(qh, ql, qh, ql, keep(th, tl))

            def couple(i, rows, out):
                shifted[rows] = out
            product(th, tl, mh, ml, couple)
            for i in range(2):
                rows, factor = factor_of(i, shifted[pl.ds(i * half_rows, half_rows)])
                th[rows], tl[rows] = split(factor)

    for copy in started:
        copy.wait_send()


def local(grad_parts, owner_order, step_count, stat_old, root_old):
    slots = jnp.arange(NB, dtype=jnp.int32)
    inverse = jnp.sum(jnp.where(owner_order[None, :] == slots[:, None], slots[None, :], 0), axis=1)
    smem = pl.BlockSpec(memory_space=pltpu.SMEM)
    vmem = pl.BlockSpec(memory_space=pltpu.VMEM)
    hbm = pl.BlockSpec(memory_space=pl.ANY)
    sem = pltpu.SemaphoreType.DMA
    square = pltpu.VMEM((W, W), BF16)
    return pl.pallas_call(
        kernel,
        out_shape=(
            jax.ShapeDtypeStruct((NB, ROWS, W), BF16),
            jax.ShapeDtypeStruct((1, W, W), F32),
            jax.ShapeDtypeStruct((1, W, W), BF16),
        ),
        in_specs=[smem, smem, smem, vmem, hbm, hbm],
        out_specs=(vmem, vmem, vmem),
        scratch_shapes=[
            pltpu.VMEM((2, NZ, ROWS, CA), BF16),
            pltpu.VMEM((2, NZ, ROWS, CA), BF16),
            pltpu.VMEM((2, NZ, 3, ROWS, CA), F32),
            pltpu.VMEM((2, NZ, 3, ROWS, CA), F32),
            pltpu.VMEM((NZ - 1, NY, ROWS, W - CA), BF16),
            pltpu.VMEM((NZ - 1, NY, ROWS, W - CA), BF16),
            pltpu.VMEM((NY, ROWS, W - CA), F32),
            pltpu.VMEM((NY - 1, ROWS, W - CA), F32),
            pltpu.VMEM((NZ - 1, ROWS, CA), F32),
            pltpu.VMEM((NZ - 1, ROWS, CA), F32),
            pltpu.VMEM((ROWS, W), F32),
            pltpu.VMEM((8, 128), F32),
            pltpu.VMEM((15, 8, 128), F32),
            pltpu.VMEM((16, ROWS, W), F32),
            pltpu.VMEM((W, W), F32),
            pltpu.VMEM((W, W), BF16),
            pltpu.VMEM((NB, ROWS, W), BF16),
            square, square, square, square, square, square, square, square,
            pltpu.VMEM((W, W), F32),
            sem((2, NZ, 4)), sem((2, NZ, 4)),
            sem((NZ - 1,)), sem((NZ - 1,)),
            sem((NY - 1,)), sem((NY - 1,)),
            sem((NZ - 1,)), sem((NZ - 1,)),
            sem((15,)), sem((15,)),
            sem((2, 4)), sem((2, 4)),
            sem((2, 4)), sem((2, 4)),
            sem, sem,
            sem((NZ - 1,)), sem((NZ - 1,)),
            sem((2, NZ, 4)), sem((2, NZ, 4)),
            sem((2,)),
        ],
        compiler_params=pltpu.CompilerParams(
            collective_id=0, has_side_effects=True, vmem_limit_bytes=48 * 2**20
        ),
        name="shampoo_step",
    )(owner_order, inverse, step_count, grad_parts, stat_old, root_old)


def solution(mesh):
    placed = (
        P("replica", None, "group", None),
        P(),
        P(),
        P("replica", None, None),
        P("replica", None, None),
    )
    return jax.shard_map(
        local,
        mesh=mesh,
        in_specs=placed,
        out_specs=(P(None, "group", None), P("replica", None, None), P("replica", None, None)),
        check_vma=False,
    )
```

time: 865 us -> 105 us (0.12)
  the two profiles are of different devices: /device:TPU:4 before, /device:TPU:1 now
where the time goes in v1:
time: 105 us
  Pallas kernels  96.9 us (92%)
  local copies, waits for them, and re-layouts  5.83 us (6%)
  between operations  1.3 us (1%)
    pallas_call x1, Pallas kernels, local(): pl.pallas_call(kernel, out_shape=(jax.ShapeDtypeStruct((NB, ROWS, W), BF1...  96.9 us
    unnamed x9, local copies, waits for them, and re-layouts  5.83 us

profile of v1, /device:TPU:1, one launch (start us, length us, event | category | flops | bytes accessed | tf_op | source)
XLA Modules:
  0.0 104.8 jit_solution(7559924442044047200)
XLA Ops:
  1.3 0.8 select_reduce_fusion.inverse
  2.0 0.0 copy-start
  2.1 1.2 %copy-done = f32[1,512,512]{2,1,0:T(8,128)S(1)} copy-done((f32[1,512,512]{2,1,0:T(8,128)S(1)}, f32[1,512,512]{2,1,0:T(8,128)}, u32[]{:S(2)}) %copy-start) | copy-done | bytes 1048600
  3.3 0.0 copy-start.1
  3.3 1.0 copy-done.1
  4.3 0.0 copy-start.2
  4.3 0.7 copy-done.2
  5.0 96.9 %shampoo_step.1 = (bf16[48,32,512]{2,1,0:T(8,128)(2,1)S(1)}, f32[1,512,512]{2,1,0:T(8,128)S(1)}, bf16[1,512,512]{2,1,0:T(8,128)(2,1)S(1)}) custom-call(s32[48]{0:T(128)S(1)} %copy-done.2, s32[48]{0:T(128)S(1)} %select_reduce_fusion.inverse, s32[1]{0:T(128)S(6)} %copy.11.step, bf16[1,48,32,512]{3,2,1,0:T(8,128)(2,1)} %gp.1, f32[1,512,512]{2,1,0:T(8,128)S(1)} %copy-done, ...), custom_call_target="tpu_custom_call" | custom-call | tf_op jit(solution)/shard_map/shampoo_step/pallas_call | solution.py:315
  101.9 1.1 %copy.12 = bf16[48,32,512]{2,1,0:T(8,128)(2,1)} copy(bf16[48,32,512]{2,1,0:T(8,128)(2,1)S(1)} %get-tuple-element.6) | data formatting | bytes 3145728
  103.0 1.0 copy.13
  104.0 0.8 copy.14
Async XLA Ops:
  2.0 1.2 %copy-start = (f32[1,512,512]{2,1,0:T(8,128)S(1)}, f32[1,512,512]{2,1,0:T(8,128)}, u32[]{:S(2)}) copy-start(f32[1,512,512]{2,1,0:T(8,128)} %stat_hbm.1) | copy-start | bytes 3145732
  3.3 1.0 copy-start.1
  4.3 0.7 copy-start.2

commit v2 on v1

v2 whole, which is shorter than its diff:
```python
import jax
import jax.numpy as jnp
from jax import lax
from jax.experimental import pallas as pl
from jax.experimental.pallas import tpu as pltpu
from jax.sharding import PartitionSpec as P

ITERS = 3
DECAY = 0.95
EPS = 0.001
NY, NZ = 8, 6
NB, ROWS, W = 48, 32, 512
SPLIT_K = 3
NORM_ORDER = (10, 11, 14, 15, 2, 3, 6, 7, 8, 9, 12, 13, 4, 5, 1)
AT_ACROSS, AT_FAR, AT_ACROSS_FAR, AT_WORK = 2, 8, 20, 24
CA = 384
F32, BF16 = jnp.float32, jnp.bfloat16


def split(value):
    high = value.astype(BF16)
    return high, (value - high.astype(F32)).astype(BF16)


def eye_block(first, rows):
    row = lax.broadcasted_iota(jnp.int32, (rows, W), 0) + first
    return row == lax.broadcasted_iota(jnp.int32, (rows, W), 1)


FAR = ((5, 4, 3, 2, 1, 0), (5, 4, 3, 0, 2, 1), (5, 0, 4, 1, 3, 2), (0, 5, 1, 4, 2, 3), (0, 1, 2, 5, 3, 4), (0, 1, 2, 3, 4, 5))
RING = (
    (0, 5, 0), (1, 5, 0), (0, 4, 0), (1, 4, 0), (0, 3, 0), (1, 3, 0), (0, 2, 0), (1, 2, 0), (0, 5, 1), (1, 5, 1),
    (0, 1, 0), (1, 1, 0), (0, 0, 0), (1, 0, 0), (0, 4, 1), (1, 3, 1), (0, 2, 1), (1, 2, 1), (0, 3, 1), (1, 4, 1),
    (0, 1, 1), (1, 1, 1), (0, 0, 1), (1, 0, 1), (0, 4, 2), (1, 3, 2), (1, 5, 2), (0, 2, 2), (1, 2, 2), (0, 3, 2),
    (0, 1, 2), (1, 1, 2), (0, 0, 2), (1, 0, 2), (0, 4, 3), (1, 3, 3), (0, 2, 3), (1, 4, 2), (0, 5, 2), (1, 5, 3),
    (1, 1, 3), (0, 0, 3),
)


def kernel(
    step, order_hbm, gp_hbm, stat_hbm, root_hbm,
    gathered, stat_out, root_out,
    order, gp,
    raw_y, raw_y_in, sum_y, sum_y_in, raw_z, raw_z_in, tot_z, tot_z_in, fin_z, fin_z_in,
    owned, norms, norms_in, rows_all, stat_v, root_v,
    th, tl, mh, ml, qh, ql, xh, xl, shifted,
    y_s, y_r, zr_s, zr_r, zt_s, zt_r, zf_s, zf_r, nb_s, nb_r, gx_s, gx_r, gc_s, gc_r, gz_s, gz_r,
    cz_s, cz_r, cy_s, cy_r, loc,
):
    gp_copy = pltpu.make_async_copy(gp_hbm.at[0], gp, loc.at[2])
    order_copy = pltpu.make_async_copy(order_hbm, order, loc.at[3])
    order_copy.start()
    gp_copy.start()
    g, r = lax.axis_index("group"), lax.axis_index("replica")
    x, zh, c = g // 4, lax.rem(g // 2, 2), lax.rem(g, 2)
    z, y = r // NY, lax.rem(r, NY)
    is_z = [(NZ - lax.rem(z + NZ - v, NZ)) // NZ for v in range(NZ)]
    row = [sum(FAR[v][k] * is_z[v] for v in range(NZ)) for k in range(NZ - 1)] + [z]

    def gid(xx, hh, cc):
        return xx * 4 + hh * 2 + cc

    def yy(d):
        return lax.rem(y + d + NY, NY)

    def at_y(d):
        return g, z * NY + yy(d)

    def at_z(k):
        return g, row[k] * NY + y

    started = []

    def describe(src, dst, ss, rs, dev):
        return pltpu.make_async_remote_copy(
            src_ref=src, dst_ref=dst, send_sem=ss, recv_sem=rs,
            device_id=dev, device_id_type=pl.DeviceIdType.MESH,
        )

    def put(src, dst, ss, rs, dev):
        copy = describe(src, dst, ss, rs, dev)
        copy.start()
        started.append(copy)

    def arrived(dst, ss, rs, dev):
        describe(dst, dst, ss, rs, dev).wait_recv()

    stat_copy = pltpu.make_async_copy(stat_hbm.at[0], stat_v, loc.at[0])
    root_copy = pltpu.make_async_copy(root_hbm.at[0], root_v, loc.at[1])
    barrier = pltpu.get_barrier_semaphore()
    peers = [at_y(d) for d in range(1, NY)] + [at_z(k) for k in range(NZ - 1)]
    peers += [(lax.bitwise_xor(g, m), r) for m in range(1, 16)]
    for dev in peers:
        pl.semaphore_signal(barrier, inc=1, device_id=dev, device_id_type=pl.DeviceIdType.MESH)
    stat_copy.start()
    root_copy.start()
    order_copy.wait()
    gp_copy.wait()

    def block(k, d, first, width):
        return gp[order[row[k] * NY + yy(d)], :, pl.ds(first, width)]

    def reach(way, k):
        return 4 if (way + k) % 2 == 0 else 3

    step_of = (1, -1)
    for k in range(NZ):
        for way in range(2):
            raw_y[way, k] = block(k, step_of[way] * reach(way, k), 0, CA)
    for k in range(NZ - 1):
        for d in range(NY):
            raw_z[k, d] = block(k, d, CA, W - CA)
    pl.semaphore_wait(barrier, len(peers))

    def near(way):
        return at_y(step_of[way])

    for k in range(NZ):
        for way in range(2):
            at = reach(way, k) - 1
            put(raw_y.at[way, k], raw_y_in.at[way, k], y_s.at[way, k, at], y_r.at[way, k, at], near(way))
    for k in range(NZ - 1):
        put(raw_z.at[k], raw_z_in.at[z], zr_s.at[k], zr_r.at[z], at_z(k))

    def incoming(way, k, d):
        if d == reach(way, k):
            arrived(raw_y_in.at[way, k], y_s.at[way, k, d - 1], y_r.at[way, k, d - 1], near(way))
            return raw_y_in[way, k].astype(F32)
        arrived(sum_y_in.at[way, k, d - 1], y_s.at[way, k, d - 1], y_r.at[way, k, d - 1], near(way))
        return sum_y_in[way, k, d - 1]

    def pass_on(d, ks=range(NZ)):
        for k in ks:
            for way in range(2):
                if d < reach(way, k):
                    total = incoming(way, k, d + 1) + block(k, step_of[way] * d, 0, CA).astype(F32)
                    sum_y[way, k, d - 1] = total
                    put(sum_y.at[way, k, d - 1], sum_y_in.at[way, k, d - 1], y_s.at[way, k, d - 1], y_r.at[way, k, d - 1], near(way))

    def totals():
        for k in range(NZ - 2, -1, -1):
            arrived(raw_z_in.at[row[k]], zr_s.at[k], zr_r.at[row[k]], at_z(k))
        for d in (4, 3, 5, 2, 6, 1, 7, 0):
            total = block(NZ - 1, d, CA, W - CA).astype(F32)
            for k in range(NZ - 1):
                total += raw_z_in[row[k], d].astype(F32)
            tot_z[d] = total
            if d:
                put(tot_z.at[d], tot_z_in.at[d - 1], zt_s.at[d - 1], zt_r.at[d - 1], at_y(d))

    pass_on(3)
    pass_on(2)
    pass_on(1, range(SPLIT_K))
    totals()
    pass_on(1, range(SPLIT_K, NZ))
    for k in range(NZ):
        total = incoming(0, k, 1) + incoming(1, k, 1) + block(k, 0, 0, CA).astype(F32)
        if k < NZ - 1:
            fin_z[k] = total
            put(fin_z.at[k], fin_z_in.at[z], zf_s.at[k], zf_r.at[z], at_z(k))
        else:
            owned[:, 0:CA] = total
    mine = tot_z[0]
    for d in range(NY - 1):
        arrived(tot_z_in.at[d], zt_s.at[d], zt_r.at[d], at_y(1))
        mine += tot_z_in[d]
    owned[:, CA:W] = mine
    mine = owned[:, 0:CA]
    for k in range(NZ - 1):
        arrived(fin_z_in.at[row[k]], zf_s.at[k], zf_r.at[row[k]], at_z(k))
        mine += fin_z_in[row[k]]
    owned[:, 0:CA] = mine

    root_copy.wait()
    products = jnp.dot(owned[...].astype(BF16), root_v[...], preferred_element_type=F32)
    mine = owned[...]
    grad_norm = jnp.sum(jnp.sum(mine * mine, axis=1, keepdims=True), axis=0, keepdims=True)
    update_norm = jnp.sum(jnp.sum(products * products, axis=1, keepdims=True), axis=0, keepdims=True)
    upper = lax.broadcasted_iota(jnp.int32, (8, 128), 0) < 4
    norms[...] = jnp.where(upper, grad_norm, update_norm)
    for m in NORM_ORDER:
        put(norms, norms_in.at[m - 1], nb_s.at[m - 1], nb_r.at[m - 1], (lax.bitwise_xor(g, m), r))

    rows_all[g] = mine

    def xat(m):
        return lax.rem(x + m, 4)

    far, sib = gid(x, 1 - zh, c), gid(x, zh, 1 - c)
    put(rows_all.at[g], rows_all.at[g], gz_s, gz_r, (far, r))
    for m in (1, 3, 2):
        put(rows_all.at[g], rows_all.at[g], gx_s.at[0, m], gx_r.at[0, m], (gid(xat(m), zh, c), r))
    put(rows_all.at[g], rows_all.at[g], gc_s.at[0, 0], gc_r.at[0, 0], (sib, r))

    total = norms[...]
    for m in range(15):
        arrived(norms_in.at[m], nb_s.at[m], nb_r.at[m], (sib, r))
        total += norms_in[m]
    graft = jnp.sqrt(total[0:1, 0:1] / (total[4:5, 0:1] + 1e-06))
    own_slot = z * NY + y
    gathered[own_slot] = (graft * products).astype(BF16)

    for k in range(NZ - 1):
        put(gathered.at[own_slot], gathered.at[own_slot], cz_s.at[k], cz_r.at[z], at_z(k))

    def slot_from(k, way, hops):
        return gathered.at[row[k] * NY + yy(-step_of[way] * hops)]

    def hop(way, k, h):
        ref = slot_from(k, way, h)
        if h:
            arrived(ref, cy_s.at[way, k, h - 1], cy_r.at[way, k, h - 1], near(way))
        elif way == 0 and k < NZ - 1:
            arrived(gathered.at[row[k] * NY + y], cz_s.at[k], cz_r.at[row[k]], at_z(k))
        if h < reach(way, k):
            put(ref, ref, cy_s.at[way, k, h], cy_r.at[way, k, h], near(way))

    def rows_from(half, m, cc):
        hh = zh if half == 0 else 1 - zh
        return rows_all.at[gid(lax.rem(x + 4 - m, 4), hh, cc)]

    def across(half):
        def go():
            for m in (1, 3, 2):
                ref = rows_from(half, m, c)
                arrived(ref, gx_s.at[half, m], gx_r.at[half, m], (sib, r))
                put(ref, ref, gc_s.at[half, m], gc_r.at[half, m], (sib, r))
        return go

    def far_rows():
        ref = rows_all.at[far]
        arrived(ref, gz_s, gz_r, (far, r))
        for m in (1, 3, 2):
            put(ref, ref, gx_s.at[1, m], gx_r.at[1, m], (gid(xat(m), zh, c), r))
        put(ref, ref, gc_s.at[1, 0], gc_r.at[1, 0], (sib, r))

    def all_rows():
        stat_copy.wait()
        for half in range(2):
            for m in range(4):
                arrived(rows_from(half, m, 1 - c), gc_s.at[half, m], gc_r.at[half, m], (sib, r))
        th[...], tl[...] = split(rows_all[...].reshape(16 * ROWS, W))

    half_rows = W // 2
    halves = [pl.ds(i * half_rows, half_rows) for i in range(2)]

    def rows_dot(a, b):
        return lax.dot_general(a, b, (((0,), (0,)), ((), ())), preferred_element_type=F32)

    def statistic(i):
        def go():
            rows = halves[i]
            gram = rows_dot(th[:, rows], th[...]) + rows_dot(th[:, rows], tl[...]) + rows_dot(tl[:, rows], th[...])
            stat_new = DECAY * stat_v[rows] + (1.0 - DECAY) * gram
            stat_out[0, rows] = stat_new
            count = step[0]
            power = jnp.float32(1.0)
            for n in range(12):
                power = jnp.where(n < count, power * DECAY, power)
            correction = 1.0 / (1.0 - jnp.full((8, 128), power, F32))
            shifted[rows] = stat_new * correction[0:1, 0:1] + jnp.where(eye_block(i * half_rows, half_rows), EPS, 0.0)
        return go

    def frobenius():
        value = shifted[...]
        return jnp.sqrt(jnp.sum(jnp.sum(value * value, axis=1, keepdims=True), axis=0, keepdims=True))

    def factor_from(i, coupled):
        rows = halves[i]
        mh[rows], ml[rows] = split(coupled)
        th[rows], tl[rows] = split((jnp.where(eye_block(i * half_rows, half_rows), 5.0, 0.0) - coupled) * 0.25)

    norm_of = []

    def start_newton():
        norm_of.append(frobenius())
        for i in range(2):
            factor_from(i, shifted[halves[i]] / norm_of[0])
            xh[halves[i]], xl[halves[i]] = th[halves[i]], tl[halves[i]]

    def product(a_high, a_low, b_high, b_low, give):
        def piece(i):
            def go():
                rows = halves[i]
                out = jnp.dot(a_high[rows], b_high[...], preferred_element_type=F32)
                out += jnp.dot(a_high[rows], b_low[...], preferred_element_type=F32)
                out += jnp.dot(a_low[rows], b_high[...], preferred_element_type=F32)
                give(i, rows, out)
            return go
        return [piece(0), piece(1)]

    def keep(high_ref, low_ref):
        def give(i, rows, out):
            high_ref[rows], low_ref[rows] = split(out)
        return give

    def couple(i, rows, out):
        shifted[rows] = out

    def next_factor():
        for i in range(2):
            factor_from(i, shifted[halves[i]])

    def take_x():
        xh[...], xl[...] = qh[...], ql[...]

    def finish(i, rows, out):
        root_out[0, rows] = (out / jnp.sqrt(jnp.sqrt(norm_of[0]))).astype(BF16)

    work = [all_rows, statistic(0), statistic(1), start_newton]
    for repeat in range(ITERS):
        last = repeat + 1 == ITERS
        if repeat:
            work += product(xh, xl, th, tl, finish if last else keep(qh, ql))
            if not last:
                work.append(take_x)
        if not last:
            work += product(th, tl, th, tl, keep(qh, ql))
            work += product(qh, ql, qh, ql, keep(th, tl))
            work += product(th, tl, mh, ml, couple)
            work.append(next_factor)

    ends = [(way, k, reach(way, k)) for k in (3, 2, 4, 5, 1, 0) for way in range(2)]
    for place, (way, k, h) in enumerate(RING + tuple(ends)):
        if place == AT_ACROSS:
            across(0)()
        if place == AT_FAR:
            far_rows()
        if place == AT_ACROSS_FAR:
            across(1)()
        if place >= AT_WORK and work:
            work.pop(0)()
        hop(way, k, h)
    for piece in work:
        piece()

    for copy in started:
        copy.wait_send()


def place_kernel(order, slots, stat, root, update, stat_out, root_out, sems):
    def update_copy(j):
        return pltpu.make_async_copy(slots.at[j], update.at[order[j]], sems.at[j])

    others = [
        pltpu.make_async_copy(stat, stat_out, sems.at[NB]),
        pltpu.make_async_copy(root, root_out, sems.at[NB + 1]),
    ]
    for copy in others:
        copy.start()
    for j in range(NB):
        update_copy(j).start()
    for copy in others:
        copy.wait()
    for j in range(NB):
        update_copy(j).wait()


def local(grad_parts, owner_order, step_count, stat_old, root_old):
    smem = pl.BlockSpec(memory_space=pltpu.SMEM)
    vmem = pl.BlockSpec(memory_space=pltpu.VMEM)
    hbm = pl.BlockSpec(memory_space=pltpu.HBM)
    sem = pltpu.SemaphoreType.DMA
    square = pltpu.VMEM((W, W), BF16)
    shapes = (
        jax.ShapeDtypeStruct((NB, ROWS, W), BF16),
        jax.ShapeDtypeStruct((1, W, W), F32),
        jax.ShapeDtypeStruct((1, W, W), BF16),
    )
    slots, stat_new, root_new = pl.pallas_call(
        kernel,
        out_shape=shapes,
        in_specs=[smem, hbm, hbm, hbm, hbm],
        out_specs=(vmem, vmem, vmem),
        scratch_shapes=[
            pltpu.SMEM((NB,), jnp.int32),
            pltpu.VMEM((NB, ROWS, W), BF16),
            pltpu.VMEM((2, NZ, ROWS, CA), BF16),
            pltpu.VMEM((2, NZ, ROWS, CA), BF16),
            pltpu.VMEM((2, NZ, 3, ROWS, CA), F32),
            pltpu.VMEM((2, NZ, 3, ROWS, CA), F32),
            pltpu.VMEM((NZ - 1, NY, ROWS, W - CA), BF16),
            pltpu.VMEM((NZ, NY, ROWS, W - CA), BF16),
            pltpu.VMEM((NY, ROWS, W - CA), F32),
            pltpu.VMEM((NY - 1, ROWS, W - CA), F32),
            pltpu.VMEM((NZ - 1, ROWS, CA), F32),
            pltpu.VMEM((NZ, ROWS, CA), F32),
            pltpu.VMEM((ROWS, W), F32),
            pltpu.VMEM((8, 128), F32),
            pltpu.VMEM((15, 8, 128), F32),
            pltpu.VMEM((16, ROWS, W), F32),
            pltpu.VMEM((W, W), F32),
            pltpu.VMEM((W, W), BF16),
            square, square, square, square, square, square, square, square,
            pltpu.VMEM((W, W), F32),
            sem((2, NZ, 4)), sem((2, NZ, 4)),
            sem((NZ - 1,)), sem((NZ,)),
            sem((NY - 1,)), sem((NY - 1,)),
            sem((NZ - 1,)), sem((NZ,)),
            sem((15,)), sem((15,)),
            sem((2, 4)), sem((2, 4)),
            sem((2, 4)), sem((2, 4)),
            sem, sem,
            sem((NZ - 1,)), sem((NZ,)),
            sem((2, NZ, 4)), sem((2, NZ, 4)),
            sem((4,)),
        ],
        compiler_params=pltpu.CompilerParams(
            collective_id=0, has_side_effects=True, vmem_limit_bytes=48 * 2**20
        ),
        name="shampoo_step",
    )(step_count, *(pltpu.with_memory_space_constraint(a, pltpu.HBM) for a in (owner_order, grad_parts, stat_old, root_old)))
    return pl.pallas_call(
        place_kernel,
        out_shape=shapes,
        in_specs=[smem, vmem, vmem, vmem],
        out_specs=(hbm, hbm, hbm),
        scratch_shapes=[sem((NB + 2,))],
        compiler_params=pltpu.CompilerParams(vmem_limit_bytes=8 * 2**20),
        name="place",
    )(owner_order, slots, stat_new, root_new)


def solution(mesh):
    placed = (
        P("replica", None, "group", None),
        P(),
        P(),
        P("replica", None, None),
        P("replica", None, None),
    )
    return jax.shard_map(
        local,
        mesh=mesh,
        in_specs=placed,
        out_specs=(P(None, "group", None), P("replica", None, None), P("replica", None, None)),
        check_vma=False,
    )
```

time: 105 us -> 89.4 us (0.85)
  Pallas kernels: 96.9 us -> 87.9 us
  local copies, waits for them, and re-layouts: 5.83 us -> 0.01 us
    pallas_call x1 -> x2, Pallas kernels: 96.9 us -> 87.9 us  [the longest x1 85.3 us: local(): pl.pallas_call(kernel, out_shape=shapes, in_specs=[smem, hbm, hbm, hbm, h...]
    unnamed x9 -> x2, local copies, waits for them, and re-layouts: 5.83 us -> 0.01 us
where the time goes in v2:
time: 89.4 us; the launch traced here: 89.2 us
  Pallas kernels  87.9 us (98%)
  between operations  1.3 us (1%)
    pallas_call x1, Pallas kernels, local(): pl.pallas_call(kernel, out_shape=shapes, in_specs=[smem, hbm, hbm, hbm, h...  85.3 us
    pallas_call x1, Pallas kernels, local(): pl.pallas_call(place_kernel, out_shape=shapes, in_specs=[smem, vmem, vmem...  2.61 us

profile of v2, /device:TPU:1, one launch (start us, length us, event | category | flops | bytes accessed | tf_op | source)
XLA Modules:
  0.0 89.2 jit_solution(6809828709391419331)
XLA Ops:
  1.3 0.0 copy-start
  1.3 85.3 %shampoo_step.1 = (bf16[48,32,512]{2,1,0:T(8,128)(2,1)S(1)}, f32[1,512,512]{2,1,0:T(8,128)S(1)}, bf16[1,512,512]{2,1,0:T(8,128)(2,1)S(1)}) custom-call(s32[1]{0:T(128)S(6)} %copy.8.step, s32[48]{0:T(128)} %order.1, bf16[1,48,32,512]{3,2,1,0:T(8,128)(2,1)} %gp_hbm.1, f32[1,512,512]{2,1,0:T(8,128)} %stat_hbm.1, bf16[1,512,512]{2,1,0:T(8,128)(2,1)} %root_hbm.1), custom_call_target="tpu_custom_call" | custom-call | tf_op jit(solution)/shard_map/shampoo_step/pallas_call | solution.py:370
  86.6 0.0 copy-done
  86.6 2.6 %place.1 = (bf16[48,32,512]{2,1,0:T(8,128)(2,1)}, f32[1,512,512]{2,1,0:T(8,128)}, bf16[1,512,512]{2,1,0:T(8,128)(2,1)}) custom-call(s32[48]{0:T(128)S(1)} %copy-done, bf16[48,32,512]{2,1,0:T(8,128)(2,1)S(1)} %get-tuple-element.6.slots, f32[1,512,512]{2,1,0:T(8,128)S(1)} %get-tuple-element.7.stat, bf16[1,512,512]{2,1,0:T(8,128)(2,1)S(1)} %get-tuple-element.8.root), custom_call_target="tpu_custom_call" | custom-call | tf_op jit(solution)/shard_map/place/pallas_call | solution.py:413
Async XLA Ops:
  1.3 85.3 %copy-start = (s32[48]{0:T(128)S(1)}, s32[48]{0:T(128)}, u32[]{:S(2)}) copy-start(s32[48]{0:T(128)} %order.1) | copy-start | bytes 580

commit v3 on v2

--- a/solution.py
+++ b/solution.py
@@ -10,9 +10,8 @@
 EPS = 0.001
 NY, NZ = 8, 6
 NB, ROWS, W = 48, 32, 512
-SPLIT_K = 3
 NORM_ORDER = (10, 11, 14, 15, 2, 3, 6, 7, 8, 9, 12, 13, 4, 5, 1)
-AT_ACROSS, AT_FAR, AT_ACROSS_FAR, AT_WORK = 2, 8, 20, 24
+AT_ACROSS, AT_FAR, AT_ACROSS_FAR, AT_WORK = 2, 10, 22, 26
 CA = 384
 F32, BF16 = jnp.float32, jnp.bfloat16
 
@@ -129,8 +128,8 @@
         arrived(sum_y_in.at[way, k, d - 1], y_s.at[way, k, d - 1], y_r.at[way, k, d - 1], near(way))
         return sum_y_in[way, k, d - 1]
 
-    def pass_on(d, ks=range(NZ)):
-        for k in ks:
+    def pass_on(d):
+        for k in range(NZ):
             for way in range(2):
                 if d < reach(way, k):
                     total = incoming(way, k, d + 1) + block(k, step_of[way] * d, 0, CA).astype(F32)
@@ -150,9 +149,8 @@
 
     pass_on(3)
     pass_on(2)
-    pass_on(1, range(SPLIT_K))
+    pass_on(1)
     totals()
-    pass_on(1, range(SPLIT_K, NZ))
     for k in range(NZ):
         total = incoming(0, k, 1) + incoming(1, k, 1) + block(k, 0, 0, CA).astype(F32)
         if k < NZ - 1:
@@ -176,8 +174,8 @@
     mine = owned[...]
     grad_norm = jnp.sum(jnp.sum(mine * mine, axis=1, keepdims=True), axis=0, keepdims=True)
     update_norm = jnp.sum(jnp.sum(products * products, axis=1, keepdims=True), axis=0, keepdims=True)
-    upper = lax.broadcasted_iota(jnp.int32, (8, 128), 0) < 4
-    norms[...] = jnp.where(upper, grad_norm, update_norm)
+    left = lax.broadcasted_iota(jnp.int32, (1, 128), 1) < 64
+    norms[...] = jnp.where(left, grad_norm, update_norm)
     for m in NORM_ORDER:
         put(norms, norms_in.at[m - 1], nb_s.at[m - 1], nb_r.at[m - 1], (lax.bitwise_xor(g, m), r))
 
@@ -196,7 +194,7 @@
     for m in range(15):
         arrived(norms_in.at[m], nb_s.at[m], nb_r.at[m], (sib, r))
         total += norms_in[m]
-    graft = jnp.sqrt(total[0:1, 0:1] / (total[4:5, 0:1] + 1e-06))
+    graft = jnp.sqrt(total[:, 0:1] / (total[:, 64:65] + 1e-06))
     own_slot = z * NY + y
     gathered[own_slot] = (graft * products).astype(BF16)
 
@@ -386,8 +384,8 @@
             pltpu.VMEM((NZ - 1, ROWS, CA), F32),
             pltpu.VMEM((NZ, ROWS, CA), F32),
             pltpu.VMEM((ROWS, W), F32),
-            pltpu.VMEM((8, 128), F32),
-            pltpu.VMEM((15, 8, 128), F32),
+            pltpu.VMEM((1, 128), F32),
+            pltpu.VMEM((15, 1, 128), F32),
             pltpu.VMEM((16, ROWS, W), F32),
             pltpu.VMEM((W, W), F32),
             pltpu.VMEM((W, W), BF16),

time: 89.4 us -> 86.8 us (0.971)
  Pallas kernels: 87.9 us -> 85.3 us
    pallas_call x1, Pallas kernels: 85.3 us -> 82.7 us  [local(): pl.pallas_call(kernel, out_shape=shapes, in_specs=[smem, hbm, hbm, hbm, h...]
where the time goes in v3:
time: 86.8 us; the launch traced here: 86.6 us
  Pallas kernels  85.3 us (98%)
  between operations  1.3 us (1%)
    pallas_call x1, Pallas kernels, local(): pl.pallas_call(kernel, out_shape=shapes, in_specs=[smem, hbm, hbm, hbm, h...  82.7 us
    pallas_call x1, Pallas kernels, local(): pl.pallas_call(place_kernel, out_shape=shapes, in_specs=[smem, vmem, vmem...  2.61 us

profile of v3, /device:TPU:1, one launch (start us, length us, event | category | flops | bytes accessed | tf_op | source)
XLA Modules:
  0.0 86.6 jit_solution(4247127086309188888)
XLA Ops:
  1.3 0.0 copy-start
  1.3 82.7 %shampoo_step.1 = (bf16[48,32,512]{2,1,0:T(8,128)(2,1)S(1)}, f32[1,512,512]{2,1,0:T(8,128)S(1)}, bf16[1,512,512]{2,1,0:T(8,128)(2,1)S(1)}) custom-call(s32[1]{0:T(128)S(6)} %copy.8.step, s32[48]{0:T(128)} %order.1, bf16[1,48,32,512]{3,2,1,0:T(8,128)(2,1)} %gp_hbm.1, f32[1,512,512]{2,1,0:T(8,128)} %stat_hbm.1, bf16[1,512,512]{2,1,0:T(8,128)(2,1)} %root_hbm.1), custom_call_target="tpu_custom_call" | custom-call | tf_op jit(solution)/shard_map/shampoo_step/pallas_call | solution.py:368
  84.0 0.0 copy-done
  84.0 2.6 %place.1 = (bf16[48,32,512]{2,1,0:T(8,128)(2,1)}, f32[1,512,512]{2,1,0:T(8,128)}, bf16[1,512,512]{2,1,0:T(8,128)(2,1)}) custom-call(s32[48]{0:T(128)S(1)} %copy-done, bf16[48,32,512]{2,1,0:T(8,128)(2,1)S(1)} %get-tuple-element.6.slots, f32[1,512,512]{2,1,0:T(8,128)S(1)} %get-tuple-element.7.stat, bf16[1,512,512]{2,1,0:T(8,128)(2,1)S(1)} %get-tuple-element.8.root), custom_call_target="tpu_custom_call" | custom-call | tf_op jit(solution)/shard_map/place/pallas_call | solution.py:411
Async XLA Ops:
  1.3 82.7 %copy-start = (s32[48]{0:T(128)S(1)}, s32[48]{0:T(128)}, u32[]{:S(2)}) copy-start(s32[48]{0:T(128)} %order.1) | copy-start | bytes 580

commit v4 on v3

--- a/solution.py
+++ b/solution.py
@@ -5,13 +5,12 @@
 from jax.experimental.pallas import tpu as pltpu
 from jax.sharding import PartitionSpec as P
 
-ITERS = 3
 DECAY = 0.95
 EPS = 0.001
 NY, NZ = 8, 6
 NB, ROWS, W = 48, 32, 512
 NORM_ORDER = (10, 11, 14, 15, 2, 3, 6, 7, 8, 9, 12, 13, 4, 5, 1)
-AT_ACROSS, AT_FAR, AT_ACROSS_FAR, AT_WORK = 2, 10, 22, 26
+AT_ACROSS, AT_NEAR, AT_FAR, AT_ACROSS_FAR, AT_WORK = 2, 6, 10, 22, 26
 CA = 384
 F32, BF16 = jnp.float32, jnp.bfloat16
 
@@ -232,23 +231,38 @@
             put(ref, ref, gx_s.at[1, m], gx_r.at[1, m], (gid(xat(m), zh, c), r))
         put(ref, ref, gc_s.at[1, 0], gc_r.at[1, 0], (sib, r))
 
-    def all_rows():
-        stat_copy.wait()
-        for half in range(2):
+    def take_rows(half):
+        def go():
             for m in range(4):
                 arrived(rows_from(half, m, 1 - c), gc_s.at[half, m], gc_r.at[half, m], (sib, r))
-        th[...], tl[...] = split(rows_all[...].reshape(16 * ROWS, W))
+            for xx in range(4):
+                rows = pl.ds((4 * half + xx) * 2 * ROWS, 2 * ROWS)
+                pair = rows_all[pl.ds(gid(xx, zh if half == 0 else 1 - zh, 0), 2)]
+                th[rows], tl[rows] = split(pair.reshape(2 * ROWS, W))
+        return go
 
     half_rows = W // 2
     halves = [pl.ds(i * half_rows, half_rows) for i in range(2)]
 
     def rows_dot(a, b):
         return lax.dot_general(a, b, (((0,), (0,)), ((), ())), preferred_element_type=F32)
+
+    def gram_of(half, i):
+        some, rows = halves[half], halves[i]
+        gram = rows_dot(th[some, rows], th[some]) + rows_dot(th[some, rows], tl[some])
+        return gram + rows_dot(tl[some, rows], th[some])
+
+    def near_gram(i):
+        def go():
+            shifted[halves[i]] = gram_of(0, i)
+        return go
 
     def statistic(i):
         def go():
             rows = halves[i]
-            gram = rows_dot(th[:, rows], th[...]) + rows_dot(th[:, rows], tl[...]) + rows_dot(tl[:, rows], th[...])
+            gram = shifted[rows] + gram_of(1, i)
+            if i == 0:
+                stat_copy.wait()
             stat_new = DECAY * stat_v[rows] + (1.0 - DECAY) * gram
             stat_out[0, rows] = stat_new
             count = step[0]
@@ -263,18 +277,18 @@
         value = shifted[...]
         return jnp.sqrt(jnp.sum(jnp.sum(value * value, axis=1, keepdims=True), axis=0, keepdims=True))
 
-    def factor_from(i, coupled):
+    def factor_from(i, coupled, high, low, keep_coupled=True):
         rows = halves[i]
-        mh[rows], ml[rows] = split(coupled)
-        th[rows], tl[rows] = split((jnp.where(eye_block(i * half_rows, half_rows), 5.0, 0.0) - coupled) * 0.25)
+        if keep_coupled:
+            mh[rows], ml[rows] = split(coupled)
+        high[rows], low[rows] = split((jnp.where(eye_block(i * half_rows, half_rows), 5.0, 0.0) - coupled) * 0.25)
 
     norm_of = []
 
     def start_newton():
         norm_of.append(frobenius())
         for i in range(2):
-            factor_from(i, shifted[halves[i]] / norm_of[0])
-            xh[halves[i]], xl[halves[i]] = th[halves[i]], tl[halves[i]]
+            factor_from(i, shifted[halves[i]] / norm_of[0], xh, xl)
 
     def product(a_high, a_low, b_high, b_low, give):
         def piece(i):
@@ -295,33 +309,30 @@
     def couple(i, rows, out):
         shifted[rows] = out
 
-    def next_factor():
-        for i in range(2):
-            factor_from(i, shifted[halves[i]])
-
-    def take_x():
-        xh[...], xl[...] = qh[...], ql[...]
+    def next_factor(keep_coupled):
+        def go():
+            for i in range(2):
+                factor_from(i, shifted[halves[i]], th, tl, keep_coupled)
+        return go
 
     def finish(i, rows, out):
         root_out[0, rows] = (out / jnp.sqrt(jnp.sqrt(norm_of[0]))).astype(BF16)
 
-    work = [all_rows, statistic(0), statistic(1), start_newton]
-    for repeat in range(ITERS):
-        last = repeat + 1 == ITERS
-        if repeat:
-            work += product(xh, xl, th, tl, finish if last else keep(qh, ql))
-            if not last:
-                work.append(take_x)
-        if not last:
-            work += product(th, tl, th, tl, keep(qh, ql))
-            work += product(qh, ql, qh, ql, keep(th, tl))
-            work += product(th, tl, mh, ml, couple)
-            work.append(next_factor)
+    work = [take_rows(1), statistic(0), statistic(1), start_newton]
+    work += product(xh, xl, xh, xl, keep(qh, ql)) + product(qh, ql, qh, ql, keep(th, tl))
+    work += product(th, tl, mh, ml, couple) + [next_factor(True)]
+    work += product(xh, xl, th, tl, keep(qh, ql)) + product(th, tl, th, tl, keep(xh, xl))
+    work += product(xh, xl, xh, xl, keep(th, tl)) + product(th, tl, mh, ml, couple) + [next_factor(False)]
+    work += product(qh, ql, th, tl, finish)
 
     ends = [(way, k, reach(way, k)) for k in (3, 2, 4, 5, 1, 0) for way in range(2)]
     for place, (way, k, h) in enumerate(RING + tuple(ends)):
         if place == AT_ACROSS:
             across(0)()
+        if place == AT_NEAR:
+            take_rows(0)()
+        if place in (AT_NEAR + 1, AT_NEAR + 2):
+            near_gram(place - AT_NEAR - 1)()
         if place == AT_FAR:
             far_rows()
         if place == AT_ACROSS_FAR:

time: 86.8 us -> 87 us (level)
  no operation moved by 1% of the time
where the time goes in v4:
time: 87 us; the launch traced here: 86.8 us
  Pallas kernels  85.5 us (98%)
  between operations  1.3 us (1%)
    pallas_call x1, Pallas kernels, local(): pl.pallas_call(kernel, out_shape=shapes, in_specs=[smem, hbm, hbm, hbm, h...  82.9 us
    pallas_call x1, Pallas kernels, local(): pl.pallas_call(place_kernel, out_shape=shapes, in_specs=[smem, vmem, vmem...  2.61 us

profile of v4, /device:TPU:1, one launch (start us, length us, event | category | flops | bytes accessed | tf_op | source)
XLA Modules:
  0.0 86.8 jit_solution(13799483289708778286)
XLA Ops:
  1.3 0.0 copy-start
  1.3 82.9 %shampoo_step.1 = (bf16[48,32,512]{2,1,0:T(8,128)(2,1)S(1)}, f32[1,512,512]{2,1,0:T(8,128)S(1)}, bf16[1,512,512]{2,1,0:T(8,128)(2,1)S(1)}) custom-call(s32[1]{0:T(128)S(6)} %copy.8.step, s32[48]{0:T(128)} %order.1, bf16[1,48,32,512]{3,2,1,0:T(8,128)(2,1)} %gp_hbm.1, f32[1,512,512]{2,1,0:T(8,128)} %stat_hbm.1, bf16[1,512,512]{2,1,0:T(8,128)(2,1)} %root_hbm.1), custom_call_target="tpu_custom_call" | custom-call | tf_op jit(solution)/shard_map/shampoo_step/pallas_call | solution.py:379
  84.2 0.0 copy-done
  84.2 2.6 %place.1 = (bf16[48,32,512]{2,1,0:T(8,128)(2,1)}, f32[1,512,512]{2,1,0:T(8,128)}, bf16[1,512,512]{2,1,0:T(8,128)(2,1)}) custom-call(s32[48]{0:T(128)S(1)} %copy-done, bf16[48,32,512]{2,1,0:T(8,128)(2,1)S(1)} %get-tuple-element.6.slots, f32[1,512,512]{2,1,0:T(8,128)S(1)} %get-tuple-element.7.stat, bf16[1,512,512]{2,1,0:T(8,128)(2,1)S(1)} %get-tuple-element.8.root), custom_call_target="tpu_custom_call" | custom-call | tf_op jit(solution)/shard_map/place/pallas_call | solution.py:422
Async XLA Ops:
  1.3 82.9 %copy-start = (s32[48]{0:T(128)S(1)}, s32[48]{0:T(128)}, u32[]{:S(2)}) copy-start(s32[48]{0:T(128)} %order.1) | copy-start | bytes 580

commit v5 on v4

--- a/solution.py
+++ b/solution.py
@@ -149,8 +149,9 @@
     pass_on(3)
     pass_on(2)
     pass_on(1)
-    totals()
     for k in range(NZ):
+        if k == NZ // 2:
+            totals()
         total = incoming(0, k, 1) + incoming(1, k, 1) + block(k, 0, 0, CA).astype(F32)
         if k < NZ - 1:
             fin_z[k] = total

time: 87 us -> 87.2 us (level)
  no operation moved by 1% of the time
where the time goes in v5:
time: 87.2 us; the launch traced here: 87.1 us
  Pallas kernels  85.8 us (98%)
  between operations  1.3 us (1%)
    pallas_call x1, Pallas kernels, local(): pl.pallas_call(kernel, out_shape=shapes, in_specs=[smem, hbm, hbm, hbm, h...  83.2 us
    pallas_call x1, Pallas kernels, local(): pl.pallas_call(place_kernel, out_shape=shapes, in_specs=[smem, vmem, vmem...  2.61 us

profile of v5, /device:TPU:1, one launch (start us, length us, event | category | flops | bytes accessed | tf_op | source)
XLA Modules:
  0.0 87.1 jit_solution(12308470602114591034)
XLA Ops:
  1.3 0.0 copy-start
  1.3 83.2 %shampoo_step.1 = (bf16[48,32,512]{2,1,0:T(8,128)(2,1)S(1)}, f32[1,512,512]{2,1,0:T(8,128)S(1)}, bf16[1,512,512]{2,1,0:T(8,128)(2,1)S(1)}) custom-call(s32[1]{0:T(128)S(6)} %copy.8.step, s32[48]{0:T(128)} %order.1, bf16[1,48,32,512]{3,2,1,0:T(8,128)(2,1)} %gp_hbm.1, f32[1,512,512]{2,1,0:T(8,128)} %stat_hbm.1, bf16[1,512,512]{2,1,0:T(8,128)(2,1)} %root_hbm.1), custom_call_target="tpu_custom_call" | custom-call | tf_op jit(solution)/shard_map/shampoo_step/pallas_call | solution.py:380
  84.5 0.0 copy-done
  84.5 2.6 %place.1 = (bf16[48,32,512]{2,1,0:T(8,128)(2,1)}, f32[1,512,512]{2,1,0:T(8,128)}, bf16[1,512,512]{2,1,0:T(8,128)(2,1)}) custom-call(s32[48]{0:T(128)S(1)} %copy-done, bf16[48,32,512]{2,1,0:T(8,128)(2,1)S(1)} %get-tuple-element.6.slots, f32[1,512,512]{2,1,0:T(8,128)S(1)} %get-tuple-element.7.stat, bf16[1,512,512]{2,1,0:T(8,128)(2,1)S(1)} %get-tuple-element.8.root), custom_call_target="tpu_custom_call" | custom-call | tf_op jit(solution)/shard_map/place/pallas_call | solution.py:423
Async XLA Ops:
  1.3 83.2 %copy-start = (s32[48]{0:T(128)S(1)}, s32[48]{0:T(128)}, u32[]{:S(2)}) copy-start(s32[48]{0:T(128)} %order.1) | copy-start | bytes 580
